TPU v7x, 256 devices: a whole 4x4x8 slice. The times are simulated.
256 devices in a mesh: own: 32 (over y, x, core), grp: 8 (over z).
Axes of the slice: x: 4, y: 4, z: 8, core: 2. Of those that a mesh axis runs over, the one named last changes fastest.
Arguments:
- embeddings: bfloat16 [262144, 768], P(('own', 'grp')), may hold values from -6 to 6
- cluster_ids: int32 [262144], P(('own', 'grp')), may hold values from 0 to 511, never falling along the last dimension, each value on 1 to 2048 neighbouring positions
Outputs:
- nearest: float32 [262144], P(('own', 'grp'))
Inputs may be any that keep to these rules, and one draw needn't show every extreme that they name: cluster_ids never falls along the rows; every cluster has 1 to 2048 rows and some cluster has exactly 2048.
All inputs are finite; a program needn't handle non-finite values.
Results may differ from a plain program's by a relative error of at most 0.0014.
Values may be sent and summed in bfloat16 or wider, within the bound.
A program may use at most 64 MiB of HBM per device.

v0:
```python
import jax
import jax.numpy as jnp
from jax import lax
from jax.sharding import PartitionSpec as P

SPAN = 2


def from_behind(block, axis, distance):
    devices = range(lax.axis_size(axis))
    route = [(i - distance, i) for i in devices if i - distance in devices]
    return lax.ppermute(block, axis, route)


def unit_rows(block):
    values = block.astype(jnp.float32)
    scale = lax.rsqrt(jnp.mean(values * values, axis=1, keepdims=True) + 1e-06)
    return (values * scale * values.shape[1] ** (-0.5)).astype(jnp.bfloat16)


def tile_maxima(left, left_ids, right, right_ids, diagonal):
    scores = lax.dot_general(
        left, right, (((1,), (1,)), ((), ())), preferred_element_type=jnp.float32
    )
    match = left_ids[:, None] == right_ids[None, :]
    if diagonal:
        rank = jnp.arange(left.shape[0], dtype=jnp.int32)
        match = match & (rank[:, None] != rank[None, :])
    masked = jnp.where(match, scores, -1.0)
    return (jnp.max(masked, axis=1), jnp.max(masked, axis=0))


def guarded(left, left_ids, right, right_ids, valid):
    hit = valid & (left_ids[-1] == right_ids[0])

    def compute():
        return tile_maxima(left, left_ids, right, right_ids, False)

    def nothing():
        return (
            jnp.full((left.shape[0],), -1.0, jnp.float32),
            jnp.full((right.shape[0],), -1.0, jnp.float32),
        )

    return lax.cond(hit, compute, nothing)


def per_device(embeddings, cluster_ids):
    unit = unit_rows(embeddings)
    count = lax.axis_size(("own", "grp"))
    place = lax.axis_index(("own", "grp"))
    best, unused = tile_maxima(unit, cluster_ids, unit, cluster_ids, True)
    for step in range(1, SPAN + 1):
        earlier, earlier_ids = from_behind((unit, cluster_ids), ("own", "grp"), step)
        row_max, col_max = guarded(earlier, earlier_ids, unit, cluster_ids, place >= step)
        returned = from_behind(row_max, ("own", "grp"), -step)
        returned = jnp.where(place + step < count, returned, -1.0)
        best = jnp.maximum(best, jnp.maximum(col_max, returned))
    return best


def solution(mesh):
    in_specs = (P(("own", "grp"), None), P(("own", "grp")))
    out_specs = P(("own", "grp"))
    return jax.shard_map(
        per_device, mesh=mesh, in_specs=in_specs, out_specs=out_specs, check_vma=False
    )
```

profile of v0, /device:TPU:24, one launch (start us, length us, event | category | flops | bytes accessed | tf_op | source)
XLA Modules:
  0.0 131.6 jit_solution(3791518069884899251)
XLA Ops:
  0.0 0.0 copy-start
  0.0 1.9 %fusion.5 = f32[1024]{0:T(1024)S(1)} fusion(bf16[1024,768]{1,0:T(8,128)(2,1)} %param.6), kind=kLoop, calls=%fused_computation.11 | loop fusion | flops 2358272 | bytes 1576960 | tf_op jit(solution)/shard_map/reduce_sum | solution.py:17
  1.9 0.0 copy-done
  1.9 0.0 copy-start.1
  1.9 0.4 fusion.7
  2.4 3.8 %collective-permute-start.1 = (bf16[1024,768]{1,0:T(8,128)(2,1)S(1)}, bf16[1024,768]{1,0:T(8,128)(2,1)}, u32[]{:S(2)}, u32[]{:S(2)}) collective-permute-start(bf16[1024,768]{1,0:T(8,128)(2,1)S(1)} %fusion.7), channel_id=1, source_target_pairs={{0,1},{1,2},{2,3},{3,4},{4,5},{5,6},{6,7},{7,8},{8,9},{9,10},{10,1... | collective-permute-start | bytes 4718600 | tf_op jit(solution)/shard_map/ppermute | solution.py:12
  6.2 5.2 %collective-permute-start.4 = (bf16[1024,768]{1,0:T(8,128)(2,1)S(1)}, bf16[1024,768]{1,0:T(8,128)(2,1)S(1)}, u32[]{:S(2)}, u32[]{:S(2)}) collective-permute-start(bf16[1024,768]{1,0:T(8,128)(2,1)S(1)} %fusion.7), channel_id=1, source_target_pairs={{0,2},{1,3},{2,4},{3,5},{4,6},{5,7},{6,8},{7,9},{8,10},{9,11},{10,... | collective-permute-start | bytes 4718600 | tf_op jit(solution)/shard_map/ppermute | solution.py:12
  11.4 0.0 copy-done.1
  11.4 5.0 %collective-permute-start = (s32[1024]{0:T(1024)S(1)}, s32[1024]{0:T(1024)S(1)}, u32[]{:S(2)}, u32[]{:S(2)}) collective-permute-start(s32[1024]{0:T(1024)S(1)} %copy-done.1), channel_id=1, source_target_pairs={{0,1},{1,2},{2,3},{3,4},{4,5},{5,6},{6,7},{7,8},{8,9},{9,10},{10,1... | collective-permute-start | bytes 12296 | tf_op jit(solution)/shard_map/ppermute | solution.py:12
  16.4 3.4 %collective-permute-start.3 = (s32[1024]{0:T(1024)S(1)}, s32[1024]{0:T(1024)S(1)}, u32[]{:S(2)}, u32[]{:S(2)}) collective-permute-start(s32[1024]{0:T(1024)S(1)} %copy-done.1), channel_id=1, source_target_pairs={{0,2},{1,3},{2,4},{3,5},{4,6},{5,7},{6,8},{7,9},{8,10},{9,11},{10,... | collective-permute-start | bytes 12296 | tf_op jit(solution)/shard_map/ppermute | solution.py:12
  19.8 0.5 slice.11
  20.4 93.3 %collective-permute-done = s32[1024]{0:T(1024)S(1)} collective-permute-done((s32[1024]{0:T(1024)S(1)}, s32[1024]{0:T(1024)S(1)}, u32[]{:S(2)}, u32[]{:S(2)}) %collective-permute-start) | collective-permute-done | bytes 4128 | tf_op jit(solution)/shard_map/ppermute | solution.py:12
  113.7 0.6 slice.10
  115.5 0.0 collective-permute-done.3
  115.5 0.6 slice.12
  117.4 0.0 collective-permute-done.1
  117.4 3.4 %conditional.2 = (f32[1024]{0:T(1024)S(1)}, f32[1024]{0:T(1024)S(1)}) conditional(s32[]{:T(128)} %convert_element_type.14, () %tuple.21, (s32[1024]{0:T(1024)S(1)}, s32[1024]{0:T(1024)S(1)}, bf16[1024,768]{1,0:T(8,128)(2,1)}, bf16[1024,768]{1,0:T(8,128)(2,1)S(1)}) %tuple.31), branch_computations={%region_2.3_spmd, %region_3.6_spmd} | conditional | flops 1614804992 | bytes 3162128 | solution.py:45
  117.4 3.3 %fusion = (f32[1024]{0:T(1024)S(1)}, f32[1024]{0:T(1024)S(1)}) fusion(s32[1024]{0:T(1024)S(1)} %get-tuple-element.22, s32[1024]{0:T(1024)S(1)} %get-tuple-element.21, bf16[1024,768]{1,0:T(8,128)(2,1)} %get-tuple-element.23, bf16[1024,768]{1,0:T(8,128)(2,1)S(1)} %get-tuple-element.24), kind=kOutput, calls=%fused_computation.1 | convolution fusion | flops 1614804992 | bytes 3162112 | tf_op jit(solution)/shard_map/cond/branch_1_fun/dot_general | solution.py:22
  120.7 1.9 %collective-permute-start.2 = (f32[1024]{0:T(1024)S(1)}, f32[1024]{0:T(1024)S(1)}, u32[]{:S(2)}, u32[]{:S(2)}) collective-permute-start(f32[1024]{0:T(1024)S(1)} %get-tuple-element.34), channel_id=1, source_target_pairs={{1,0},{2,1},{3,2},{4,3},{5,4},{6,5},{7,6},{8,7},{9,8},{10,9},{11,1... | collective-permute-start | bytes 12296 | tf_op jit(solution)/shard_map/ppermute | solution.py:12
  122.6 0.0 collective-permute-done.4
  122.7 2.0 %conditional.3 = (f32[1024]{0:T(1024)S(1)}, f32[1024]{0:T(1024)S(1)}) conditional(s32[]{:T(128)} %convert_element_type.15, () %tuple.23, (s32[1024]{0:T(1024)S(1)}, s32[1024]{0:T(1024)S(1)}, bf16[1024,768]{1,0:T(8,128)(2,1)S(1)}, bf16[1024,768]{1,0:T(8,128)(2,1)S(1)}) %tuple.32), branch_computations={%region_6.7_spmd, %region_7.10_spmd} | conditional | flops 1614804992 | bytes 3162128 | solution.py:45
  122.7 1.9 %fusion.2 = (f32[1024]{0:T(1024)S(1)}, f32[1024]{0:T(1024)S(1)}) fusion(s32[1024]{0:T(1024)S(1)} %get-tuple-element.26, s32[1024]{0:T(1024)S(1)} %get-tuple-element.25, bf16[1024,768]{1,0:T(8,128)(2,1)S(1)} %get-tuple-element.27, bf16[1024,768]{1,0:T(8,128)(2,1)S(1)} %get-tuple-element.28), kind=kOutput, calls=%fused_computation.4 | convolution fusion | flops 1614804992 | bytes 3162112 | tf_op jit(solution)/shard_map/cond/branch_1_fun/dot_general | solution.py:22
  124.6 2.2 %collective-permute-start.5 = (f32[1024]{0:T(1024)S(1)}, f32[1024]{0:T(1024)S(1)}, u32[]{:S(2)}, u32[]{:S(2)}) collective-permute-start(f32[1024]{0:T(1024)S(1)} %get-tuple-element.36), channel_id=1, source_target_pairs={{2,0},{3,1},{4,2},{5,3},{6,4},{7,5},{8,6},{9,7},{10,8},{11,9},{12,... | collective-permute-start | bytes 12296 | tf_op jit(solution)/shard_map/ppermute | solution.py:12
  126.8 2.0 %select_reduce_fusion = f32[1024]{0:T(1024)S(1)} fusion(s32[1024]{0:T(1024)S(1)} %copy-done.1, bf16[1024,768]{1,0:T(8,128)(2,1)S(1)} %fusion.7), kind=kOutput, calls=%fused_computation.6 | convolution fusion | flops 1615854592 | bytes 1581056 | tf_op jit(solution)/shard_map/dot_general | solution.py:22
  128.8 0.0 collective-permute-done.2
  128.8 2.2 %collective-permute-done.5 = f32[1024]{0:T(1024)S(1)} collective-permute-done((f32[1024]{0:T(1024)S(1)}, f32[1024]{0:T(1024)S(1)}, u32[]{:S(2)}, u32[]{:S(2)}) %collective-permute-start.5) | collective-permute-done | bytes 4128 | tf_op jit(solution)/shard_map/ppermute | solution.py:12
  131.0 0.6 maximum_maximum_fusion
  (1 shorter events, 0.0 us)
Async XLA Ops:
  0.0 1.9 %copy-start = (bf16[1024,768]{1,0:T(8,128)(2,1)S(1)}, bf16[1024,768]{1,0:T(8,128)(2,1)}, u32[]{:S(2)}) copy-start(bf16[1024,768]{1,0:T(8,128)(2,1)} %param.6) | copy-start | bytes 4718596
  1.9 9.5 %copy-start.1 = (s32[1024]{0:T(1024)S(1)}, s32[1024]{0:T(1024)}, u32[]{:S(2)}) copy-start(s32[1024]{0:T(1024)} %param.7) | copy-start | bytes 12292
  2.4 115.0 %collective-permute-start.1 = (bf16[1024,768]{1,0:T(8,128)(2,1)S(1)}, bf16[1024,768]{1,0:T(8,128)(2,1)}, u32[]{:S(2)}, u32[]{:S(2)}) collective-permute-start(bf16[1024,768]{1,0:T(8,128)(2,1)S(1)} %fusion.7), channel_id=1, source_target_pairs={{0,1},{1,2},{2,3},{3,4},{4,5},{5,6},{6,7},{7,8},{8,9},{9,10},{10,1... | collective-permute-start | bytes 4718600 | tf_op jit(solution)/shard_map/ppermute | solution.py:12
  6.2 116.4 %collective-permute-start.4 = (bf16[1024,768]{1,0:T(8,128)(2,1)S(1)}, bf16[1024,768]{1,0:T(8,128)(2,1)S(1)}, u32[]{:S(2)}, u32[]{:S(2)}) collective-permute-start(bf16[1024,768]{1,0:T(8,128)(2,1)S(1)} %fusion.7), channel_id=1, source_target_pairs={{0,2},{1,3},{2,4},{3,5},{4,6},{5,7},{6,8},{7,9},{8,10},{9,11},{10,... | collective-permute-start | bytes 4718600 | tf_op jit(solution)/shard_map/ppermute | solution.py:12
  11.4 102.2 %collective-permute-start = (s32[1024]{0:T(1024)S(1)}, s32[1024]{0:T(1024)S(1)}, u32[]{:S(2)}, u32[]{:S(2)}) collective-permute-start(s32[1024]{0:T(1024)S(1)} %copy-done.1), channel_id=1, source_target_pairs={{0,1},{1,2},{2,3},{3,4},{4,5},{5,6},{6,7},{7,8},{8,9},{9,10},{10,1... | collective-permute-start | bytes 12296 | tf_op jit(solution)/shard_map/ppermute | solution.py:12
  16.4 99.1 %collective-permute-start.3 = (s32[1024]{0:T(1024)S(1)}, s32[1024]{0:T(1024)S(1)}, u32[]{:S(2)}, u32[]{:S(2)}) collective-permute-start(s32[1024]{0:T(1024)S(1)} %copy-done.1), channel_id=1, source_target_pairs={{0,2},{1,3},{2,4},{3,5},{4,6},{5,7},{6,8},{7,9},{8,10},{9,11},{10,... | collective-permute-start | bytes 12296 | tf_op jit(solution)/shard_map/ppermute | solution.py:12
  120.7 8.1 %collective-permute-start.2 = (f32[1024]{0:T(1024)S(1)}, f32[1024]{0:T(1024)S(1)}, u32[]{:S(2)}, u32[]{:S(2)}) collective-permute-start(f32[1024]{0:T(1024)S(1)} %get-tuple-element.34), channel_id=1, source_target_pairs={{1,0},{2,1},{3,2},{4,3},{5,4},{6,5},{7,6},{8,7},{9,8},{10,9},{11,1... | collective-permute-start | bytes 12296 | tf_op jit(solution)/shard_map/ppermute | solution.py:12
  124.6 6.4 %collective-permute-start.5 = (f32[1024]{0:T(1024)S(1)}, f32[1024]{0:T(1024)S(1)}, u32[]{:S(2)}, u32[]{:S(2)}) collective-permute-start(f32[1024]{0:T(1024)S(1)} %get-tuple-element.36), channel_id=1, source_target_pairs={{2,0},{3,1},{4,2},{5,3},{6,4},{7,5},{8,6},{9,7},{10,8},{11,9},{12,... | collective-permute-start | bytes 12296 | tf_op jit(solution)/shard_map/ppermute | solution.py:12
where the time goes:
time: 132 us
  waiting for transfers between devices  95.5 us (72%)
  starting transfers between devices  21.5 us (16%)
  matrix products  7.29 us (6%)
  other arithmetic  2.93 us (2%)
  between operations  2.67 us (2%)
  local copies, waits for them, and re-layouts  1.71 us (1%)
    ppermute x6, waiting for transfers between devices, from_behind(): return lax.ppermute(block, axis, route)  95.5 us
    ppermute x6, starting transfers between devices, from_behind(): return lax.ppermute(block, axis, route)  21.5 us
    dot_general x3, matrix products, tile_maxima(): lax.dot_general(left, right, (((1,), (1,)), ((), ())), preferred_element_...  7.29 us
  transfers between devices with their start and end apart: 6, of which 2 were waited for; matrix products, arithmetic and copies ran while one was open for 7% of the time, Pallas kernels for 0%

commit v1 on v0

v1 whole, which is shorter than its diff:
```python
import functools

import jax
import jax.numpy as jnp
from jax import lax
from jax.experimental import pallas as pl
from jax.experimental.pallas import tpu as pltpu
from jax.sharding import PartitionSpec as P

MESH = pl.DeviceIdType.MESH
LANES = 128
NT = (((1,), (1,)), ((), ()))


def as_columns(ids_ref, col_ref):
    for t in range(ids_ref.shape[0]):
        wide = jnp.broadcast_to(ids_ref[t : t + 1, :].astype(jnp.float32), (LANES, LANES))
        col_ref[t * LANES : (t + 1) * LANES, :] = wide.T.astype(jnp.int32)


def fold(masked):
    rows, lanes = masked.shape
    return jnp.max(masked.reshape(rows // 8, 8, lanes), axis=0)


def tile_into(acc, rows, row_ids, cols, col_ids, first, count, diagonal=None):
    scores = lax.dot_general(
        rows, cols[first * LANES : (first + count) * LANES, :], NT, preferred_element_type=jnp.float32
    )
    for t in range(count):
        part = scores[:, t * LANES : (t + 1) * LANES]
        match = row_ids == col_ids[first + t : first + t + 1, :]
        if diagonal is not None:
            rank = lax.broadcasted_iota(jnp.int32, part.shape, 0) + diagonal
            lane = lax.broadcasted_iota(jnp.int32, part.shape, 1) + (first + t) * LANES
            match = match & (rank != lane)
        where = pl.ds((first + t) * LANES, LANES)
        acc[:, where] = jnp.maximum(acc[:, where], fold(jnp.where(match, part, -1.0)))


def kernel(n, inner, x_hbm, ids, out, x, unit, lo, hi, lo_ids, hi_ids, own_col, lo_col, hi_col,
           best, for_lo, for_hi, send_lo, send_hi, from_lo, from_hi,
           load_sem, row_send, row_recv, id_send, id_recv, back_send, back_recv):
    rows, width = unit.shape
    step = LANES
    steps = rows // step
    me = lax.axis_index("own") * inner + lax.axis_index("grp")

    def at(flat):
        return (flat // inner, lax.rem(flat, inner))

    right = at(lax.rem(me + 1, n))
    left = at(lax.rem(me + n - 1, n))

    order = []
    for k in range(steps // 2):
        order += [k, steps - 1 - k]
    loads = {
        c: pltpu.make_async_copy(x_hbm.at[pl.ds(c * step, step)], x.at[pl.ds(c * step, step)], load_sem.at[c])
        for c in range(steps)
    }
    for c in order:
        loads[c].start()

    barrier = pltpu.get_barrier_semaphore()
    for target in (left, right):
        pl.semaphore_signal(barrier, inc=1, device_id=target, device_id_type=MESH)

    def remote(src, dst, send_sem, recv_sem, target):
        return pltpu.make_async_remote_copy(
            src_ref=src, dst_ref=dst, send_sem=send_sem, recv_sem=recv_sem, device_id=target, device_id_type=MESH
        )

    to_right, to_left = [], []
    for k in range(steps):
        up = pl.ds((steps - 1 - k) * step, step)
        down = pl.ds(k * step, step)
        to_right.append(remote(unit.at[up], lo.at[up], row_send.at[0, k], row_recv.at[0, k], right))
        to_left.append(remote(unit.at[down], hi.at[down], row_send.at[1, k], row_recv.at[1, k], left))
    ids_right = remote(ids, lo_ids, id_send.at[0], id_recv.at[0], right)
    ids_left = remote(ids, hi_ids, id_send.at[1], id_recv.at[1], left)

    def normalise(c):
        loads[c].wait()
        where = pl.ds(c * step, step)
        values = x[where, :].astype(jnp.float32)
        scale = lax.rsqrt(jnp.mean(values * values, axis=1, keepdims=True) + 1e-06)
        unit[where, :] = (values * scale * width ** (-0.5)).astype(jnp.bfloat16)

    for k in range(steps // 2):
        normalise(k)
        normalise(steps - 1 - k)
        if k == 0:
            pl.semaphore_wait(barrier, 2)
            ids_right.start()
            ids_left.start()
        to_right[k].start()
        to_left[k].start()
    for k in range(steps // 2, steps):
        to_right[k].start()
        to_left[k].start()

    for acc in (best, for_lo, for_hi):
        acc[...] = jnp.full(acc.shape, -1.0, jnp.float32)
    as_columns(ids, own_col)

    def own_step(c, carry):
        start = pl.multiple_of(c * step, step)
        where = pl.ds(start, step)
        tile_into(best, unit[where, :], own_col[where, :], unit, ids, 0, steps, diagonal=start)
        return carry

    lax.fori_loop(0, steps, own_step, 0)

    ids_right.wait_recv()
    as_columns(lo_ids, lo_col)
    ids_left.wait_recv()
    as_columns(hi_ids, hi_col)

    for k in range(steps):
        up = pl.ds((steps - 1 - k) * step, step)
        down = pl.ds(k * step, step)
        to_right[k].wait_recv()
        to_left[k].wait_recv()
        near = min(k, steps - 1 - k) + 1
        tile_into(for_hi, lo[up, :], lo_col[up, :], hi, hi_ids, 0, near)
        tile_into(for_lo, hi[down, :], hi_col[down, :], lo, lo_ids, steps - near, near)
        near_lo = pl.ds(rows - near * step, near * step)
        near_hi = pl.ds(0, near * step)
        tile_into(for_hi, lo[near_lo, :], lo_col[near_lo, :], hi, hi_ids, k, 1)
        tile_into(for_lo, hi[near_hi, :], hi_col[near_hi, :], lo, lo_ids, steps - 1 - k, 1)
        if k == steps - 1:
            for t in range(steps):
                lane = pl.ds(t * LANES, LANES)
                send_lo[t : t + 1, :] = jnp.max(for_lo[:, lane], axis=0, keepdims=True)
                send_hi[t : t + 1, :] = jnp.max(for_hi[:, lane], axis=0, keepdims=True)
            back_left = remote(send_lo, from_hi, back_send.at[0], back_recv.at[0], left)
            back_right = remote(send_hi, from_lo, back_send.at[1], back_recv.at[1], right)
            back_left.start()
            back_right.start()
        tile_into(best, lo[up, :], lo_col[up, :], unit, ids, 0, steps)
        tile_into(best, hi[down, :], hi_col[down, :], unit, ids, 0, steps)

    for k in range(steps):
        to_right[k].wait_send()
        to_left[k].wait_send()
    ids_right.wait_send()
    ids_left.wait_send()
    back_left.wait()
    back_right.wait()
    for t in range(steps):
        mine = jnp.max(best[:, t * LANES : (t + 1) * LANES], axis=0, keepdims=True)
        out[t : t + 1, :] = jnp.maximum(mine, jnp.maximum(from_lo[t : t + 1, :], from_hi[t : t + 1, :]))


def solution(mesh):
    inner = mesh.shape["grp"]
    n = inner * mesh.shape["own"]

    def per_device(embeddings, cluster_ids):
        rows, width = embeddings.shape
        tiles = rows // LANES
        ids = cluster_ids.reshape(tiles, LANES)
        block = pltpu.VMEM((rows, width), jnp.bfloat16)
        few_ids = pltpu.VMEM((tiles, LANES), jnp.int32)
        col = pltpu.VMEM((rows, LANES), jnp.int32)
        acc = pltpu.VMEM((8, rows), jnp.float32)
        small = pltpu.VMEM((tiles, LANES), jnp.float32)
        dma = pltpu.SemaphoreType.DMA
        out = pl.pallas_call(
            functools.partial(kernel, n, inner),
            out_shape=jax.ShapeDtypeStruct((tiles, LANES), jnp.float32),
            in_specs=[pl.BlockSpec(memory_space=pltpu.HBM), pl.BlockSpec(memory_space=pltpu.VMEM)],
            out_specs=pl.BlockSpec(memory_space=pltpu.VMEM),
            scratch_shapes=[block] * 4 + [few_ids] * 2 + [col] * 3 + [acc] * 3 + [small] * 4
            + [dma((tiles,)), dma((2, tiles)), dma((2, tiles)), dma((2,)), dma((2,)), dma((2,)), dma((2,))],
            compiler_params=pltpu.CompilerParams(
                collective_id=0, has_side_effects=True, vmem_limit_bytes=48 * 1024 * 1024
            ),
        )(embeddings, ids)
        return out.reshape(rows)

    return jax.shard_map(
        per_device,
        mesh=mesh,
        in_specs=(P(("own", "grp"), None), P(("own", "grp"))),
        out_specs=P(("own", "grp")),
        check_vma=False,
    )
```

time: 132 us -> 53.2 us (0.40)
  waiting for transfers between devices: 95.5 us -> 0 us
  Pallas kernels: 0 us -> 50.4 us
  starting transfers between devices: 21.5 us -> 0 us
  matrix products: 7.29 us -> 0 us
  other arithmetic: 2.93 us -> 0 us
  between operations: 2.67 us -> 0.01 us
    ppermute x6 -> x0, waiting for transfers between devices: 95.5 us -> none  [from_behind(): return lax.ppermute(block, axis, route)]
    pallas_call x0 -> x1, Pallas kernels: none -> 50.4 us  [per_device(): pl.pallas_call(functools.partial(kernel, n, inner), out_shape=jax.ShapeDt...]
    ppermute x6 -> x0, starting transfers between devices: 21.5 us -> none  [from_behind(): return lax.ppermute(block, axis, route)]
    dot_general x3 -> x0, matrix products: 7.29 us -> none  [tile_maxima(): lax.dot_general(left, right, (((1,), (1,)), ((), ())), preferred_element_...]
    unnamed x4 -> x5, local copies, waits for them, and re-layouts: 0.01 us -> 2.69 us
    reduce_sum x1 -> x0, other arithmetic: 1.9 us -> none  [unit_rows(): scale = lax.rsqrt(jnp.mean(values * values, axis=1, keepdims=True) + 1e-06)]
    slice x3 -> x0, local copies, waits for them, and re-layouts: 1.7 us -> none  [guarded(): hit = valid & (left_ids[-1] == right_ids[0])]
  transfers between devices with their start and end apart: 6 -> 0, of which waited for: 2 -> 0; matrix products, arithmetic and copies ran while one was open for 7% -> 0% of each run, Pallas kernels for 0% -> 0%
where the time goes in v1:
time: 53.2 us; the launch traced here: 53.1 us
  Pallas kernels  50.4 us (95%)
  local copies, waits for them, and re-layouts  2.69 us (5%)
    pallas_call x1, Pallas kernels, per_device(): pl.pallas_call(functools.partial(kernel, n, inner), out_shape=jax.ShapeDt...  50.4 us
    unnamed x5, local copies, waits for them, and re-layouts  2.69 us

profile of v1, /device:TPU:24, one launch (start us, length us, event | category | flops | bytes accessed | tf_op | source)
XLA Modules:
  0.0 53.1 jit_solution(15195612137974999184)
XLA Ops:
  0.0 0.0 copy-start
  0.0 1.4 %copy-done = bf16[1024,768]{1,0:T(8,128)(2,1)S(1)} copy-done((bf16[1024,768]{1,0:T(8,128)(2,1)S(1)}, bf16[1024,768]{1,0:T(8,128)(2,1)}, u32[]{:S(2)}) %copy-start) | copy-done | bytes 1572888
  1.4 0.0 copy-start.1
  1.4 0.7 %copy-done.1 = s32[1024]{0:T(1024)S(1)} copy-done((s32[1024]{0:T(1024)S(1)}, s32[1024]{0:T(1024)}, u32[]{:S(2)}) %copy-start.1) | copy-done | bytes 4120
  2.1 50.4 %shard_map.28 = f32[8,128]{1,0:T(8,128)S(1)} custom-call(bf16[1024,768]{1,0:T(8,128)(2,1)S(1)} %copy-done, s32[8,128]{1,0:T(8,128)S(1)} %bitcast.3), custom_call_target="tpu_custom_call" | custom-call | tf_op jit(solution)/shard_map/pallas_call | solution.py:170
  52.5 0.6 %copy.4 = f32[1024]{0:T(1024)} copy(f32[1024]{0:T(1024)S(1)} %bitcast.2) | data formatting | bytes 8192
Async XLA Ops:
  0.0 1.4 %copy-start = (bf16[1024,768]{1,0:T(8,128)(2,1)S(1)}, bf16[1024,768]{1,0:T(8,128)(2,1)}, u32[]{:S(2)}) copy-start(bf16[1024,768]{1,0:T(8,128)(2,1)} %x_hbm.1) | copy-start | bytes 4718596
  1.4 0.7 %copy-start.1 = (s32[1024]{0:T(1024)S(1)}, s32[1024]{0:T(1024)}, u32[]{:S(2)}) copy-start(s32[1024]{0:T(1024)} %param.3) | copy-start | bytes 12292

commit v2 on v1

v2 whole, which is shorter than its diff:
```python
import functools

import jax
import jax.numpy as jnp
from jax import lax
from jax.experimental import pallas as pl
from jax.experimental.pallas import tpu as pltpu
from jax.sharding import PartitionSpec as P

MESH = pl.DeviceIdType.MESH
LANES = 128
FIRST = 64
ROW = 8
HOLD = 2
LAST = 64
NT = (((1,), (1,)), ((), ()))


def as_columns(ids_ref, col_ref):
    for t in range(ids_ref.shape[0]):
        wide = jnp.broadcast_to(ids_ref[t : t + 1, :].astype(jnp.float32), (LANES, LANES))
        col_ref[t * LANES : (t + 1) * LANES, :] = wide.T.astype(jnp.int32)


def fold(masked):
    rows, lanes = masked.shape
    return jnp.max(masked.reshape(rows // 8, 8, lanes), axis=0)


def tile_into(acc, rows, row_ids, cols, col_ids, first, count, diagonal=None):
    scores = lax.dot_general(
        rows, cols[first * LANES : (first + count) * LANES, :], NT, preferred_element_type=jnp.float32
    )
    for t in range(count):
        part = scores[:, t * LANES : (t + 1) * LANES]
        match = row_ids == col_ids[first + t : first + t + 1, :]
        if diagonal is not None:
            rank = lax.broadcasted_iota(jnp.int32, part.shape, 0) + diagonal
            lane = lax.broadcasted_iota(jnp.int32, part.shape, 1) + (first + t) * LANES
            match = match & (rank != lane)
        where = pl.ds((first + t) * LANES, LANES)
        acc[:, where] = jnp.maximum(acc[:, where], fold(jnp.where(match, part, -1.0)))


def narrow(acc, small):
    for t in range(small.shape[0]):
        small[t : t + 1, :] = jnp.max(acc[:, t * LANES : (t + 1) * LANES], axis=0, keepdims=True)


def unit_rows(raw):
    values = raw.astype(jnp.float32)
    scale = lax.rsqrt(jnp.mean(values * values, axis=1, keepdims=True) + 1e-06)
    return (values * scale * values.shape[1] ** (-0.5)).astype(jnp.bfloat16)


def chunks_of(rows):
    edges = [0, FIRST] + list(range(LANES, rows - LANES + 1, LANES)) + [rows - LAST, rows]
    return list(zip(edges[:-1], edges[1:]))


def kernel(n, inner, x_hbm, ids_hbm, out, x, unit, lo, hi, ids, lo_ids, hi_ids, own_col, lo_col, hi_col,
           best, for_lo, for_hi, send_lo, send_hi, from_lo, from_hi, mine,
           load_sem, row_send, row_recv, id_load, id_send, id_recv, back_send, back_recv):
    rows, width = unit.shape
    tiles = rows // LANES
    chunks = chunks_of(rows)
    own, grp = lax.axis_index("own"), lax.axis_index("grp")
    me = own * inner + grp
    has_left, has_right = me > 0, me < n - 1
    late_right = (grp == inner - 1) & (lax.rem(own, ROW) == ROW - 2)
    late_left = (grp == 0) & (lax.rem(own, ROW) == 1)

    def at(flat):
        return (flat // inner, lax.rem(flat, inner))

    right = at(lax.rem(me + 1, n))
    left = at(lax.rem(me + n - 1, n))

    barrier = pltpu.get_barrier_semaphore()

    @pl.when(has_left)
    def _():
        pl.semaphore_signal(barrier, inc=1, device_id=left, device_id_type=MESH)

    @pl.when(has_right)
    def _():
        pl.semaphore_signal(barrier, inc=1, device_id=right, device_id_type=MESH)

    order = []
    for k in range(tiles // 2):
        order += [tiles - 1 - k, k]
    load_ids = pltpu.make_async_copy(ids_hbm, ids, id_load)
    load_ids.start()
    loads = {}
    for c in order:
        where = pl.ds(c * LANES, LANES)
        loads[c] = pltpu.make_async_copy(x_hbm.at[where], x.at[where], load_sem.at[c])
        loads[c].start()

    def remote(src, dst, send_sem, recv_sem, target):
        return pltpu.make_async_remote_copy(
            src_ref=src, dst_ref=dst, send_sem=send_sem, recv_sem=recv_sem, device_id=target, device_id_type=MESH
        )

    up = [pl.ds(rows - b, b - a) for a, b in chunks]
    down = [pl.ds(a, b - a) for a, b in chunks]
    to_right, to_left = [], []
    for k in range(len(chunks)):
        source = x_hbm if k == 0 else unit
        to_right.append(remote(source.at[up[k]], lo.at[up[k]], row_send.at[0, k], row_recv.at[0, k], right))
        to_left.append(remote(source.at[down[k]], hi.at[down[k]], row_send.at[1, k], row_recv.at[1, k], left))
    ids_right = remote(ids_hbm, lo_ids, id_send.at[0], id_recv.at[0], right)
    ids_left = remote(ids_hbm, hi_ids, id_send.at[1], id_recv.at[1], left)

    inside = has_left & has_right

    @pl.when(inside)
    def _():
        pl.semaphore_wait(barrier, 2)

    @pl.when(jnp.logical_not(inside))
    def _():
        pl.semaphore_wait(barrier, 1)

    def begin(copies, ids_copy):
        copies[0].start()
        ids_copy.start()

    def go_on(copies):
        for copy in copies[1:]:
            copy.start()

    early_right = has_right & jnp.logical_not(late_right)
    early_left = has_left & jnp.logical_not(late_left)
    pl.when(early_right)(lambda: begin(to_right, ids_right))
    pl.when(early_left)(lambda: begin(to_left, ids_left))

    def normalise(c):
        loads[c].wait()
        where = pl.ds(c * LANES, LANES)
        unit[where, :] = unit_rows(x[where, :])

    for c in order:
        normalise(c)
    pl.when(early_right)(lambda: go_on(to_right))
    pl.when(early_left)(lambda: go_on(to_left))

    for acc in (best, for_lo, for_hi):
        acc[...] = jnp.full(acc.shape, -1.0, jnp.float32)
    load_ids.wait()
    as_columns(ids, own_col)

    def own_step(c, carry):
        start = pl.multiple_of(c * LANES, LANES)
        where = pl.ds(start, LANES)
        tile_into(best, unit[where, :], own_col[where, :], unit, ids, 0, tiles, diagonal=start)
        return carry

    lax.fori_loop(0, HOLD, own_step, 0)

    @pl.when(late_right)
    def _():
        begin(to_right, ids_right)
        go_on(to_right)

    @pl.when(late_left)
    def _():
        begin(to_left, ids_left)
        go_on(to_left)

    lax.fori_loop(HOLD, tiles, own_step, 0)

    def missing(ids_ref, back):
        ids_ref[...] = jnp.full(ids_ref.shape, -1, jnp.int32)
        back[...] = jnp.full(back.shape, -1.0, jnp.float32)

    pl.when(jnp.logical_not(has_left))(lambda: missing(lo_ids, from_lo))
    pl.when(jnp.logical_not(has_right))(lambda: missing(hi_ids, from_hi))

    for k, (a, b) in enumerate(chunks):
        pl.when(has_left)(to_right[k].wait_recv)
        pl.when(has_right)(to_left[k].wait_recv)
        if k == 0:

            pl.when(has_left)(ids_right.wait_recv)
            as_columns(lo_ids, lo_col)
            pl.when(has_right)(ids_left.wait_recv)
            as_columns(hi_ids, hi_col)
            lo[up[0], :] = unit_rows(lo[up[0], :])
            hi[down[0], :] = unit_rows(hi[down[0], :])
        near = min(b // LANES, -(-(rows - a) // LANES))
        full = b // LANES - 1
        reach = min(a, rows - full * LANES) if b % LANES == 0 else 0
        lo_rows, hi_rows = pl.ds(rows - reach, reach), pl.ds(0, reach)
        if near > 0:
            tile_into(for_hi, lo[up[k], :], lo_col[up[k], :], hi, hi_ids, 0, near)
        if reach > 0:
            tile_into(for_hi, lo[lo_rows, :], lo_col[lo_rows, :], hi, hi_ids, full, 1)
        if b == rows:
            narrow(for_hi, send_hi)
            back_right = remote(send_hi, from_lo, back_send.at[1], back_recv.at[1], right)
            pl.when(has_right)(back_right.start)
        if near > 0:
            tile_into(for_lo, hi[down[k], :], hi_col[down[k], :], lo, lo_ids, tiles - near, near)
        if reach > 0:
            tile_into(for_lo, hi[hi_rows, :], hi_col[hi_rows, :], lo, lo_ids, tiles - 1 - full, 1)
        if b == rows:
            narrow(for_lo, send_lo)
            back_left = remote(send_lo, from_hi, back_send.at[0], back_recv.at[0], left)
            pl.when(has_left)(back_left.start)
        tile_into(best, lo[up[k], :], lo_col[up[k], :], unit, ids, 0, tiles)
        tile_into(best, hi[down[k], :], hi_col[down[k], :], unit, ids, 0, tiles)

    narrow(best, mine)

    @pl.when(has_right)
    def _():
        for copy in to_right + [ids_right]:
            copy.wait_send()
        back_right.wait_send()

    @pl.when(has_left)
    def _():
        for copy in to_left + [ids_left]:
            copy.wait_send()
        back_left.wait_send()

    pl.when(has_right)(back_left.wait_recv)
    pl.when(has_left)(back_right.wait_recv)
    out[...] = jnp.maximum(mine[...], jnp.maximum(from_lo[...], from_hi[...]))


def solution(mesh):
    inner = mesh.shape["grp"]
    n = inner * mesh.shape["own"]

    def per_device(embeddings, cluster_ids):
        rows, width = embeddings.shape
        tiles = rows // LANES
        parts = len(chunks_of(rows))
        ids = cluster_ids.reshape(tiles, LANES)
        block = pltpu.VMEM((rows, width), jnp.bfloat16)
        few_ids = pltpu.VMEM((tiles, LANES), jnp.int32)
        col = pltpu.VMEM((rows, LANES), jnp.int32)
        acc = pltpu.VMEM((8, rows), jnp.float32)
        small = pltpu.VMEM((tiles, LANES), jnp.float32)
        dma = pltpu.SemaphoreType.DMA
        out = pl.pallas_call(
            functools.partial(kernel, n, inner),
            out_shape=jax.ShapeDtypeStruct((tiles, LANES), jnp.float32),
            in_specs=[pl.BlockSpec(memory_space=pltpu.HBM)] * 2,
            out_specs=pl.BlockSpec(memory_space=pltpu.VMEM),
            scratch_shapes=[block] * 4 + [few_ids] * 3 + [col] * 3 + [acc] * 3 + [small] * 5
            + [dma((tiles,)), dma((2, parts)), dma((2, parts)), dma, dma((2,)), dma((2,)), dma((2,)), dma((2,))],
            compiler_params=pltpu.CompilerParams(
                collective_id=0, has_side_effects=True, vmem_limit_bytes=63 * 1024 * 1024
            ),
        )(embeddings, ids)
        return out.reshape(rows)

    return jax.shard_map(
        per_device,
        mesh=mesh,
        in_specs=(P(("own", "grp"), None), P(("own", "grp"))),
        out_specs=P(("own", "grp")),
        check_vma=False,
    )
```

time: 53.2 us -> 52.7 us (level)
  local copies, waits for them, and re-layouts: 2.69 us -> 1.28 us
  Pallas kernels: 50.4 us -> 51.3 us
    unnamed x5 -> x1, local copies, waits for them, and re-layouts: 2.69 us -> 1.28 us
    pallas_call x1, Pallas kernels: 50.4 us -> 51.3 us  [per_device(): pl.pallas_call(functools.partial(kernel, n, inner), out_shape=jax.ShapeDt...]
where the time goes in v2:
time: 52.7 us; the launch traced here: 52.6 us
  Pallas kernels  51.3 us (97%)
  local copies, waits for them, and re-layouts  1.28 us (2%)
    pallas_call x1, Pallas kernels, per_device(): pl.pallas_call(functools.partial(kernel, n, inner), out_shape=jax.ShapeDt...  51.3 us
    unnamed x1, local copies, waits for them, and re-layouts  1.28 us

profile of v2, /device:TPU:24, one launch (start us, length us, event | category | flops | bytes accessed | tf_op | source)
XLA Modules:
  0.0 52.6 jit_solution(4907314197634445755)
XLA Ops:
  0.0 51.3 %shard_map.28 = f32[8,128]{1,0:T(8,128)} custom-call(bf16[1024,768]{1,0:T(8,128)(2,1)} %x_hbm.1, s32[8,128]{1,0:T(8,128)} %bitcast.3), custom_call_target="tpu_custom_call" | custom-call | tf_op jit(solution)/shard_map/pallas_call | solution.py:248
  51.3 1.3 %copy.4 = f32[1024]{0:T(1024)} copy(f32[1024]{0:T(1024)} %bitcast.2) | data formatting | bytes 8192

commit v3 on v2

--- a/solution.py
+++ b/solution.py
@@ -11,7 +11,8 @@
 LANES = 128
 FIRST = 64
 ROW = 8
-HOLD = 2
+HOLD = 7
+RESUME = 6
 LAST = 64
 NT = (((1,), (1,)), ((), ()))
 
@@ -67,8 +68,7 @@
     own, grp = lax.axis_index("own"), lax.axis_index("grp")
     me = own * inner + grp
     has_left, has_right = me > 0, me < n - 1
-    late_right = (grp == inner - 1) & (lax.rem(own, ROW) == ROW - 2)
-    late_left = (grp == 0) & (lax.rem(own, ROW) == 1)
+    late_left = (grp == 0) & (lax.rem(own, ROW) == 1) & (own > ROW)
 
     def at(flat):
         return (flat // inner, lax.rem(flat, inner))
@@ -127,13 +127,11 @@
         ids_copy.start()
 
     def go_on(copies):
-        for copy in copies[1:]:
+        for copy in copies:
             copy.start()
 
-    early_right = has_right & jnp.logical_not(late_right)
-    early_left = has_left & jnp.logical_not(late_left)
-    pl.when(early_right)(lambda: begin(to_right, ids_right))
-    pl.when(early_left)(lambda: begin(to_left, ids_left))
+    pl.when(has_right)(lambda: begin(to_right, ids_right))
+    pl.when(has_left)(lambda: begin(to_left, ids_left))
 
     def normalise(c):
         loads[c].wait()
@@ -142,8 +140,9 @@
 
     for c in order:
         normalise(c)
-    pl.when(early_right)(lambda: go_on(to_right))
-    pl.when(early_left)(lambda: go_on(to_left))
+    pl.when(has_right)(lambda: go_on(to_right[1:]))
+    pl.when(has_left)(lambda: go_on(to_left[1:HOLD]))
+    pl.when(has_left & jnp.logical_not(late_left))(lambda: go_on(to_left[HOLD:]))
 
     for acc in (best, for_lo, for_hi):
         acc[...] = jnp.full(acc.shape, -1.0, jnp.float32)
@@ -156,19 +155,7 @@
         tile_into(best, unit[where, :], own_col[where, :], unit, ids, 0, tiles, diagonal=start)
         return carry
 
-    lax.fori_loop(0, HOLD, own_step, 0)
-
-    @pl.when(late_right)
-    def _():
-        begin(to_right, ids_right)
-        go_on(to_right)
-
-    @pl.when(late_left)
-    def _():
-        begin(to_left, ids_left)
-        go_on(to_left)
-
-    lax.fori_loop(HOLD, tiles, own_step, 0)
+    lax.fori_loop(0, tiles, own_step, 0)
 
     def missing(ids_ref, back):
         ids_ref[...] = jnp.full(ids_ref.shape, -1, jnp.int32)
@@ -180,6 +167,8 @@
     for k, (a, b) in enumerate(chunks):
         pl.when(has_left)(to_right[k].wait_recv)
         pl.when(has_right)(to_left[k].wait_recv)
+        if k == RESUME:
+            pl.when(late_left)(lambda: go_on(to_left[HOLD:]))
         if k == 0:
 
             pl.when(has_left)(ids_right.wait_recv)

time: 52.7 us -> 49 us (0.930)
  the two profiles are of different devices: /device:TPU:24 before, /device:TPU:9 now
where the time goes in v3:
time: 49 us; the launch traced here: 48.9 us
  Pallas kernels  47.6 us (97%)
  local copies, waits for them, and re-layouts  1.28 us (3%)
    pallas_call x1, Pallas kernels, per_device(): pl.pallas_call(functools.partial(kernel, n, inner), out_shape=jax.ShapeDt...  47.6 us
    unnamed x1, local copies, waits for them, and re-layouts  1.28 us

profile of v3, /device:TPU:9, one launch (start us, length us, event | category | flops | bytes accessed | tf_op | source)
XLA Modules:
  0.0 48.9 jit_solution(6679579857093005096)
XLA Ops:
  0.0 47.6 %shard_map.28 = f32[8,128]{1,0:T(8,128)} custom-call(bf16[1024,768]{1,0:T(8,128)(2,1)} %x_hbm.1, s32[8,128]{1,0:T(8,128)} %bitcast.3), custom_call_target="tpu_custom_call" | custom-call | tf_op jit(solution)/shard_map/pallas_call | solution.py:237
  47.6 1.3 %copy.4 = f32[1024]{0:T(1024)} copy(f32[1024]{0:T(1024)} %bitcast.2) | data formatting | bytes 8192

commit v4 on v3

--- a/solution.py
+++ b/solution.py
@@ -13,7 +13,7 @@
 ROW = 8
 HOLD = 7
 RESUME = 6
-LAST = 64
+LAST = 128
 NT = (((1,), (1,)), ((), ()))
 
 
@@ -55,7 +55,7 @@
 
 
 def chunks_of(rows):
-    edges = [0, FIRST] + list(range(LANES, rows - LANES + 1, LANES)) + [rows - LAST, rows]
+    edges = [0, FIRST] + list(range(LANES, rows + 1, LANES))
     return list(zip(edges[:-1], edges[1:]))
 
 
@@ -78,13 +78,13 @@
 
     barrier = pltpu.get_barrier_semaphore()
 
+    @pl.when(has_right)
+    def _():
+        pl.semaphore_signal(barrier, inc=1, device_id=right, device_id_type=MESH)
+
     @pl.when(has_left)
     def _():
         pl.semaphore_signal(barrier, inc=1, device_id=left, device_id_type=MESH)
-
-    @pl.when(has_right)
-    def _():
-        pl.semaphore_signal(barrier, inc=1, device_id=right, device_id_type=MESH)
 
     order = []
     for k in range(tiles // 2):
@@ -123,15 +123,15 @@
         pl.semaphore_wait(barrier, 1)
 
     def begin(copies, ids_copy):
+        ids_copy.start()
         copies[0].start()
-        ids_copy.start()
 
     def go_on(copies):
         for copy in copies:
             copy.start()
 
+    pl.when(has_left)(lambda: begin(to_left, ids_left))
     pl.when(has_right)(lambda: begin(to_right, ids_right))
-    pl.when(has_left)(lambda: begin(to_left, ids_left))
 
     def normalise(c):
         loads[c].wait()

time: 49 us -> 48.7 us (level)
  the two profiles are of different devices: /device:TPU:9 before, /device:TPU:24 now
where the time goes in v4:
time: 48.7 us; the launch traced here: 47.8 us
  Pallas kernels  46.5 us (95%)
  local copies, waits for them, and re-layouts  1.28 us (3%)
    pallas_call x1, Pallas kernels, per_device(): pl.pallas_call(functools.partial(kernel, n, inner), out_shape=jax.ShapeDt...  46.5 us
    unnamed x1, local copies, waits for them, and re-layouts  1.28 us

profile of v4, /device:TPU:24, one launch (start us, length us, event | category | flops | bytes accessed | tf_op | source)
XLA Modules:
  0.0 47.8 jit_solution(17682136727900003835)
XLA Ops:
  0.0 46.5 %shard_map.28 = f32[8,128]{1,0:T(8,128)} custom-call(bf16[1024,768]{1,0:T(8,128)(2,1)} %x_hbm.1, s32[8,128]{1,0:T(8,128)} %bitcast.3), custom_call_target="tpu_custom_call" | custom-call | tf_op jit(solution)/shard_map/pallas_call | solution.py:237
  46.6 1.3 %copy.4 = f32[1024]{0:T(1024)} copy(f32[1024]{0:T(1024)} %bitcast.2) | data formatting | bytes 8192

commit v5 on v4

--- a/solution.py
+++ b/solution.py
@@ -166,6 +166,9 @@
 
     for k, (a, b) in enumerate(chunks):
         pl.when(has_left)(to_right[k].wait_recv)
+        near = min(b // LANES, -(-(rows - a) // LANES))
+        if 0 < near * LANES <= a:
+            tile_into(for_hi, lo[up[k], :], lo_col[up[k], :], hi, hi_ids, 0, near)
         pl.when(has_right)(to_left[k].wait_recv)
         if k == RESUME:
             pl.when(late_left)(lambda: go_on(to_left[HOLD:]))
@@ -177,11 +180,10 @@
             as_columns(hi_ids, hi_col)
             lo[up[0], :] = unit_rows(lo[up[0], :])
             hi[down[0], :] = unit_rows(hi[down[0], :])
-        near = min(b // LANES, -(-(rows - a) // LANES))
         full = b // LANES - 1
         reach = min(a, rows - full * LANES) if b % LANES == 0 else 0
         lo_rows, hi_rows = pl.ds(rows - reach, reach), pl.ds(0, reach)
-        if near > 0:
+        if near > 0 and near * LANES > a:
             tile_into(for_hi, lo[up[k], :], lo_col[up[k], :], hi, hi_ids, 0, near)
         if reach > 0:
             tile_into(for_hi, lo[lo_rows, :], lo_col[lo_rows, :], hi, hi_ids, full, 1)

time: 48.7 us -> 48.6 us (level)
  the two profiles are of different devices: /device:TPU:24 before, /device:TPU:27 now
where the time goes in v5:
time: 48.6 us; the launch traced here: 48.5 us
  Pallas kernels  47.2 us (97%)
  local copies, waits for them, and re-layouts  1.28 us (3%)
    pallas_call x1, Pallas kernels, per_device(): pl.pallas_call(functools.partial(kernel, n, inner), out_shape=jax.ShapeDt...  47.2 us
    unnamed x1, local copies, waits for them, and re-layouts  1.28 us

profile of v5, /device:TPU:27, one launch (start us, length us, event | category | flops | bytes accessed | tf_op | source)
XLA Modules:
  0.0 48.5 jit_solution(4659590965443539182)
XLA Ops:
  0.0 47.2 %shard_map.28 = f32[8,128]{1,0:T(8,128)} custom-call(bf16[1024,768]{1,0:T(8,128)(2,1)} %x_hbm.1, s32[8,128]{1,0:T(8,128)} %bitcast.3), custom_call_target="tpu_custom_call" | custom-call | tf_op jit(solution)/shard_map/pallas_call | solution.py:239
  47.2 1.3 %copy.4 = f32[1024]{0:T(1024)} copy(f32[1024]{0:T(1024)} %bitcast.2) | data formatting | bytes 8192
